TPU v7x, 512 devices: a whole 4x8x8 slice. The times are simulated.
512 devices in a mesh: layer: 8 (over z), row: 64 (over x, y, core).
Axes of the slice: x: 4, y: 8, z: 8, core: 2. Of those that a mesh axis runs over, the one named last changes fastest.
Arguments:
- leaf_rhs: float32 [8, 64, 256, 384], P('layer', 'row'), may hold values from -6 to 6
- leaf_inverse: float32 [8, 64, 256, 256], P('layer', 'row'), may hold values from -0.375 to 0.375
- leaf_coupling: float32 [8, 64, 4, 512, 256], P('layer', 'row'), may hold values from -0.046875 to 0.046875
- parent: int32 [8, 64], P('layer', 'row'), may hold values from 0 to 3
- sep_rhs: float32 [8, 4, 512, 384], P('layer', None, 'row'), may hold values from -6 to 6
- sep_inverse: float32 [8, 4, 512, 512], P('layer', None, 'row'), may hold values from -0.25 to 0.25
- sep_coupling: float32 [8, 3, 512, 512], P('layer', None, 'row'), may hold values from -0.125 to 0.125
- root_coupling: float32 [8, 512, 512], P('layer', 'row'), may hold values from -0.09375 to 0.09375
- root_rhs: float32 [512, 384], P('row'), may hold values from -6 to 6
- root_inverse: float32 [512, 512], P('row'), may hold values from -0.25 to 0.25
Outputs:
- sep_solution: float32 [8, 4, 512, 384], P('layer', None, 'row')
- root_solution: float32 [512, 384], P('row')
All inputs are finite; a program needn't handle non-finite values.
Results may differ from a plain program's by a relative error of at most 0.0003.
Values sent between devices are 32-bit elements; how exact they have to be, the bound alone decides.
No kernel may reach another device: no remote copies, remote signals or barrier semaphores. Data moves between devices by JAX's collectives and lax.ppermute only.
A program may use at most 64 MiB of HBM per device.

v0:
```python
import jax
import jax.numpy as jnp
from jax import lax
from jax.sharding import PartitionSpec as P


def body(
    leaf_rhs,
    leaf_inverse,
    leaf_coupling,
    parent,
    sep_rhs,
    sep_inverse,
    sep_coupling,
    root_coupling,
    root_rhs,
    root_inverse,
):
    highest = lax.Precision.HIGHEST
    sep_count = sep_rhs.shape[1]
    row_count = sep_rhs.shape[2]
    row_start = lax.axis_index("row") * row_count
    leaf_solution = jnp.dot(leaf_inverse[0, 0], leaf_rhs[0, 0], precision=highest)
    levels = jnp.arange(sep_count, dtype=jnp.int32)
    keep_mask = (levels >= parent[0, 0]).astype(jnp.float32)
    coupled = (
        jnp.einsum("kwb,bc->kwc", leaf_coupling[0, 0], leaf_solution, precision=highest)
        * keep_mask[:, None, None]
    )
    own_rhs = lax.dynamic_update_slice_in_dim(jnp.zeros_like(coupled), sep_rhs[0], row_start, 1)
    residual = lax.psum(own_rhs - coupled, "row")
    residual_list = [residual[k] for k in range(sep_count)]
    local_rows = [
        jnp.dot(sep_inverse[0, k], residual_list[k], precision=highest) for k in range(sep_count)
    ]
    solved = []
    gathered = None
    for k in range(sep_count):
        current = local_rows[k]
        if k > 0:
            current = current - jnp.dot(sep_coupling[0, k - 1], gathered, precision=highest)
        solved.append(current)
        gathered = lax.all_gather(current, "row", axis=0, tiled=True)
    sep_out = jnp.stack(solved)[None]
    root_term = jnp.dot(root_coupling[0], gathered, precision=highest)
    root_sum = lax.psum(root_term, "layer")
    root_residual = root_rhs - root_sum
    root_out = jnp.dot(
        root_inverse, lax.all_gather(root_residual, "row", axis=0, tiled=True), precision=highest
    )
    return (sep_out, root_out)


def solution(mesh):
    return jax.shard_map(
        body,
        mesh=mesh,
        in_specs=(
            P("layer", "row", None, None),
            P("layer", "row", None, None),
            P("layer", "row", None, None, None),
            P("layer", "row"),
            P("layer", None, "row", None),
            P("layer", None, "row", None),
            P("layer", None, "row", None),
            P("layer", "row", None),
            P("row", None),
            P("row", None),
        ),
        out_specs=(P("layer", None, "row", None), P("row", None)),
        check_vma=False,
    )
```

profile of v0, /device:TPU:1, one launch (start us, length us, event | category | flops | bytes accessed | tf_op | source)
XLA Modules:
  0.0 522.9 jit_solution(4747656309365464238)
XLA Ops:
  7.2 0.0 copy-start
  7.2 0.0 all-reduce.2.cloned.1.call-start
  7.2 1.2 copy.12
  9.1 1.9 convolution_bitcast_fusion
  11.0 2.1 broadcast_in_dim.7
  13.1 4.4 dynamic_update_slice.3
  17.5 0.0 copy-done
  17.5 5.6 %bitcast_subtract_fusion = f32[4,512,384]{1,2,0:T(8,128)} fusion(f32[4,512,384]{1,2,0:T(8,128)} %dynamic_update_slice.3, f32[256,384,1]{0,1,2:T(8,128)S(1)} %convolution_bitcast_fusion, f32[1,1,4,512,256]{4,3,2,1,0:T(8,128)S(1)} %copy-done, f32[4]{0:T(128)S(1)} %compare_convert_fusion), kind=kOutput, calls=%fused_computation | convolution fusion | flops 2417491968 | bytes 8781840 | tf_op jit(solution)/shard_map/kwb,bc->kwc/dot_general | solution.py:27
  23.1 0.0 copy-start.2
  23.1 0.0 copy-start.3
  23.1 0.0 all-reduce.2.cloned.1.call-update
  23.2 207.1 %all-reduce.2.cloned.1.call-done = f32[4,512,384]{1,2,0:T(8,128)} async-done(((f32[4,512,384]{1,2,0:T(8,128)}), f32[4,512,384]{1,2,0:T(8,128)}) %all-reduce.2.cloned.1.call-update) | async-done | bytes 3145744 | tf_op jit(solution)/shard_map/psum | solution.py:31
  230.2 0.0 copy-done.2
  230.2 0.0 copy-start.1
  230.2 2.0 fusion.7
  232.2 50.8 %all_gather.15 = f32[512,384]{1,0:T(8,128)S(1)} all-gather(f32[8,384]{1,0:T(8,128)S(1)} %bitcast.80), channel_id=1, replica_groups=mesh['layer'=8,'row'=64] {'row'}, dimensions={0}, use_global_device_ids=true | all-gather | bytes 798720 | tf_op jit(solution)/shard_map/all_gather | solution.py:43
  283.0 1.8 fusion.6
  284.9 0.0 copy-done.3
  284.9 0.0 copy-start.4
  284.9 0.5 convolution_subtract_fusion.2
  285.4 0.0 copy-start.6
  285.4 48.8 %all_gather.16 = f32[512,384]{1,0:T(8,128)S(1)} all-gather(f32[8,384]{1,0:T(8,128)S(1)} %bitcast.82), channel_id=1, replica_groups=mesh['layer'=8,'row'=64] {'row'}, dimensions={0}, use_global_device_ids=true | all-gather | bytes 798720 | tf_op jit(solution)/shard_map/all_gather | solution.py:43
  334.2 0.0 copy-done.1
  334.2 0.0 copy-start.5
  334.2 0.7 fusion.5
  334.9 0.5 convolution_subtract_fusion.1
  335.5 48.9 %all_gather.17 = f32[512,384]{1,0:T(8,128)S(1)} all-gather(f32[8,384]{1,0:T(8,128)S(1)} %bitcast.84), channel_id=1, replica_groups=mesh['layer'=8,'row'=64] {'row'}, dimensions={0}, use_global_device_ids=true | all-gather | bytes 798720 | tf_op jit(solution)/shard_map/all_gather | solution.py:43
  384.3 0.7 fusion.4
  385.1 0.5 convolution_subtract_fusion
  385.6 48.7 %all_gather.18 = f32[512,384]{1,0:T(8,128)S(1)} all-gather(f32[8,384]{1,0:T(8,128)S(1)} %bitcast.86), channel_id=1, replica_groups=mesh['layer'=8,'row'=64] {'row'}, dimensions={0}, use_global_device_ids=true | all-gather | bytes 798720 | tf_op jit(solution)/shard_map/all_gather | solution.py:43
  434.3 0.0 copy-done.4
  434.3 0.5 convolution_bitcast_fusion.2
  434.8 23.6 %psum.15 = f32[8,384]{1,0:T(8,128)S(1)} all-reduce(f32[8,384]{1,0:T(8,128)S(1)} %convolution_bitcast_fusion.2), channel_id=1, replica_groups=mesh['layer'=8,'row'=64] {'layer'}, use_global_device_ids=true, to_apply=%region_1.0 | all-reduce | flops 3072 | bytes 24576 | tf_op jit(solution)/shard_map/psum | solution.py:46
  458.4 0.0 copy-done.6
  458.4 55.9 %all_gather.19 = f32[512,384]{1,0:T(8,128)S(1)} all-gather(f32[8,384]{1,0:T(8,128)S(1)} %sub.31), channel_id=1, replica_groups=mesh['layer'=8,'row'=64] {'row'}, dimensions={0}, use_global_device_ids=true | all-gather | bytes 798720 | tf_op jit(solution)/shard_map/all_gather | solution.py:49
  514.3 0.0 copy-done.5
  514.3 1.1 convolution_bitcast_fusion.1
  515.4 0.6 maximum_bitcast_fusion
  (2 shorter events, 0.0 us)
Async XLA Ops:
  7.2 10.3 %copy-start = (f32[1,1,4,512,256]{4,3,2,1,0:T(8,128)S(1)}, f32[1,1,4,512,256]{4,3,2,1,0:T(8,128)}, u32[]{:S(2)}) copy-start(f32[1,1,4,512,256]{4,3,2,1,0:T(8,128)} %param.12) | copy-start | bytes 6291460
  7.2 223.1 %all-reduce.2.cloned.1.call-start = ((), (), s32[]{:S(2)}) async-start(), calls=%async_computation | async-start | bytes 6291456 | tf_op jit(solution)/shard_map/psum | solution.py:31
  23.1 207.1 %copy-start.2 = (f32[1,4,8,512]{3,2,1,0:T(8,128)S(1)}, f32[1,4,8,512]{3,2,1,0:T(8,128)}, u32[]{:S(2)}) copy-start(f32[1,4,8,512]{3,2,1,0:T(8,128)} %param.15) | copy-start | bytes 196612
  23.1 261.7 %copy-start.3 = (f32[1,3,8,512]{3,2,1,0:T(8,128)S(1)}, f32[1,3,8,512]{3,2,1,0:T(8,128)}, u32[]{:S(2)}) copy-start(f32[1,3,8,512]{3,2,1,0:T(8,128)} %param.16) | copy-start | bytes 147460
  230.2 104.0 %copy-start.1 = (f32[4,512,384]{1,2,0:T(8,128)S(1)}, f32[4,512,384]{1,2,0:T(8,128)}, u32[]{:S(2)}) copy-start(f32[4,512,384]{1,2,0:T(8,128)} %all-reduce.2.cloned.1.call-done) | copy-start | bytes 9437188
  284.9 149.4 %copy-start.4 = (f32[1,8,512]{2,1,0:T(8,128)S(1)}, f32[1,8,512]{2,1,0:T(8,128)}, u32[]{:S(2)}) copy-start(f32[1,8,512]{2,1,0:T(8,128)} %param.17) | copy-start | bytes 49156
  285.4 173.0 %copy-start.6 = (f32[8,384]{1,0:T(8,128)S(1)}, f32[8,384]{1,0:T(8,128)}, u32[]{:S(2)}) copy-start(f32[8,384]{1,0:T(8,128)} %param.18) | copy-start | bytes 36868
  334.2 180.1 %copy-start.5 = (f32[8,512]{1,0:T(8,128)S(1)}, f32[8,512]{1,0:T(8,128)}, u32[]{:S(2)}) copy-start(f32[8,512]{1,0:T(8,128)} %param.19) | copy-start | bytes 49156
Sparse Core Ops, SparseCore 0:
  23.3 206.9 all-reduce.1
where the time goes:
time: 523 us
  blocking collectives  277 us (53%)
  waiting for transfers between devices  207 us (40%)
  matrix products  16 us (3%)
  between operations  14.8 us (3%)
  local copies, waits for them, and re-layouts  7.74 us (1%)
    psum x1, waiting for transfers between devices, body(): residual = lax.psum(own_rhs - coupled, 'row')  207 us
    all_gather x4, blocking collectives, body(): gathered = lax.all_gather(current, 'row', axis=0, tiled=True)  197 us
    all_gather x1, blocking collectives, body(): lax.all_gather(root_residual, 'row', axis=0, tiled=True)  55.9 us
    psum x1, blocking collectives, body(): root_sum = lax.psum(root_term, 'layer')  23.6 us
  transfers between devices with their start and end apart: 1, of which 1 were waited for; matrix products, arithmetic and copies ran while one was open for 0% of the time, Pallas kernels for 0%

commit v1 on v0

--- a/solution.py
+++ b/solution.py
@@ -1,7 +1,18 @@
+import functools
 import jax
 import jax.numpy as jnp
 from jax import lax
 from jax.sharding import PartitionSpec as P
+
+
+def part_stacks_all_on_mesh(arr, mesh_dim):
+    part_now = jnp.concatenate(
+        lax.all_to_all(jnp.stack([arr for _ in range(lax.psum(1, mesh_dim))], 0), mesh_dim, 0, 0), 0
+    )
+    return part_now
+
+
+attach_paths = functools.partial(part_stacks_all_on_mesh, mesh_dim="row")
 
 
 def body(
@@ -45,9 +56,7 @@
     root_term = jnp.dot(root_coupling[0], gathered, precision=highest)
     root_sum = lax.psum(root_term, "layer")
     root_residual = root_rhs - root_sum
-    root_out = jnp.dot(
-        root_inverse, lax.all_gather(root_residual, "row", axis=0, tiled=True), precision=highest
-    )
+    root_out = jnp.dot(root_inverse, attach_paths(root_residual), precision=highest)
     return (sep_out, root_out)
 
 

time: 523 us -> 506 us (0.967)
  blocking collectives: 277 us -> 221 us
  waiting for transfers between devices: 207 us -> 230 us
  starting transfers between devices: 0.04 us -> 14.9 us
    all_gather x1 -> x0, blocking collectives: 55.9 us -> none  [body(): lax.all_gather(root_residual, 'row', axis=0, tiled=True)]
    all_to_all x0 -> x1, waiting for transfers between devices: none -> 22.4 us  [part_stacks_all_on_mesh(): lax.all_to_all(jnp.stack([arr for _ in range(lax.psum(1, mesh_dim))], 0),...]
    all_to_all x0 -> x1, starting transfers between devices: none -> 14.8 us  [part_stacks_all_on_mesh(): lax.all_to_all(jnp.stack([arr for _ in range(lax.psum(1, mesh_dim))], 0),...]
  transfers between devices with their start and end apart: 1 -> 2, of which waited for: 1 -> 2; matrix products, arithmetic and copies ran while one was open for 0% -> 0% of each run, Pallas kernels for 0% -> 0%
where the time goes in v1:
time: 506 us; the launch traced here: 505 us
  waiting for transfers between devices  230 us (45%)
  blocking collectives  221 us (44%)
  matrix products  16 us (3%)
  starting transfers between devices  14.9 us (3%)
  between operations  14.8 us (3%)
  local copies, waits for them, and re-layouts  8.69 us (2%)
    psum x1, waiting for transfers between devices, body(): residual = lax.psum(own_rhs - coupled, 'row')  207 us
    all_gather x4, blocking collectives, body(): gathered = lax.all_gather(current, 'row', axis=0, tiled=True)  197 us
    psum x1, blocking collectives, body(): root_sum = lax.psum(root_term, 'layer')  23.6 us
    all_to_all x1, waiting for transfers between devices, part_stacks_all_on_mesh(): lax.all_to_all(jnp.stack([arr for _ in range(lax.psum(1, mesh_dim))], 0),...  22.4 us
    all_to_all x1, starting transfers between devices, part_stacks_all_on_mesh(): lax.all_to_all(jnp.stack([arr for _ in range(lax.psum(1, mesh_dim))], 0),...  14.8 us
  transfers between devices with their start and end apart: 2, of which 2 were waited for; matrix products, arithmetic and copies ran while one was open for 0% of the time, Pallas kernels for 0%

profile of v1, /device:TPU:1, one launch (start us, length us, event | category | flops | bytes accessed | tf_op | source)
XLA Modules:
  0.0 505.3 jit_solution(14717193746604218605)
XLA Ops:
  7.2 0.0 copy-start
  7.2 0.0 all-reduce.2.cloned.1.call-start
  7.2 1.2 copy.12
  9.1 1.9 convolution_bitcast_fusion
  11.0 2.1 broadcast_in_dim.7
  13.1 4.4 dynamic_update_slice.3
  17.5 0.0 copy-done
  17.5 5.6 %bitcast_subtract_fusion = f32[4,512,384]{1,2,0:T(8,128)} fusion(f32[4,512,384]{1,2,0:T(8,128)} %dynamic_update_slice.3, f32[256,384,1]{0,1,2:T(8,128)S(1)} %convolution_bitcast_fusion, f32[1,1,4,512,256]{4,3,2,1,0:T(8,128)S(1)} %copy-done, f32[4]{0:T(128)S(1)} %compare_convert_fusion), kind=kOutput, calls=%fused_computation | convolution fusion | flops 2417491968 | bytes 8781840 | tf_op jit(solution)/shard_map/kwb,bc->kwc/dot_general | solution.py:38
  23.1 0.0 copy-start.2
  23.1 0.0 copy-start.3
  23.1 0.0 all-reduce.2.cloned.1.call-update
  23.2 207.1 %all-reduce.2.cloned.1.call-done = f32[4,512,384]{1,2,0:T(8,128)} async-done(((f32[4,512,384]{1,2,0:T(8,128)}), f32[4,512,384]{1,2,0:T(8,128)}) %all-reduce.2.cloned.1.call-update) | async-done | bytes 3145744 | tf_op jit(solution)/shard_map/psum | solution.py:42
  230.3 0.0 copy-done.2
  230.3 0.0 copy-start.1
  230.3 2.0 fusion.7
  232.3 50.8 %all_gather.12 = f32[512,384]{1,0:T(8,128)S(1)} all-gather(f32[8,384]{1,0:T(8,128)S(1)} %bitcast.82), channel_id=1, replica_groups=mesh['layer'=8,'row'=64] {'row'}, dimensions={0}, use_global_device_ids=true | all-gather | bytes 798720 | tf_op jit(solution)/shard_map/all_gather | solution.py:54
  283.1 1.8 fusion.6
  284.9 0.0 copy-done.3
  285.0 0.0 copy-start.4
  285.0 0.5 convolution_subtract_fusion.2
  285.5 0.0 copy-start.6
  285.5 48.8 %all_gather.13 = f32[512,384]{1,0:T(8,128)S(1)} all-gather(f32[8,384]{1,0:T(8,128)S(1)} %bitcast.84), channel_id=1, replica_groups=mesh['layer'=8,'row'=64] {'row'}, dimensions={0}, use_global_device_ids=true | all-gather | bytes 798720 | tf_op jit(solution)/shard_map/all_gather | solution.py:54
  334.3 0.0 copy-done.1
  334.3 0.7 fusion.5
  335.0 0.5 convolution_subtract_fusion.1
  335.6 0.0 copy-start.5
  335.6 48.9 %all_gather.14 = f32[512,384]{1,0:T(8,128)S(1)} all-gather(f32[8,384]{1,0:T(8,128)S(1)} %bitcast.86), channel_id=1, replica_groups=mesh['layer'=8,'row'=64] {'row'}, dimensions={0}, use_global_device_ids=true | all-gather | bytes 798720 | tf_op jit(solution)/shard_map/all_gather | solution.py:54
  384.4 0.7 fusion.4
  385.1 0.5 convolution_subtract_fusion
  385.7 48.8 %all_gather.15 = f32[512,384]{1,0:T(8,128)S(1)} all-gather(f32[8,384]{1,0:T(8,128)S(1)} %bitcast.88), channel_id=1, replica_groups=mesh['layer'=8,'row'=64] {'row'}, dimensions={0}, use_global_device_ids=true | all-gather | bytes 798720 | tf_op jit(solution)/shard_map/all_gather | solution.py:54
  434.4 0.0 copy-done.4
  434.4 0.5 convolution_bitcast_fusion.2
  434.9 23.6 %psum.15 = f32[8,384]{1,0:T(8,128)S(1)} all-reduce(f32[8,384]{1,0:T(8,128)S(1)} %convolution_bitcast_fusion.2), channel_id=1, replica_groups=mesh['layer'=8,'row'=64] {'layer'}, use_global_device_ids=true, to_apply=%region_1.0 | all-reduce | flops 3072 | bytes 24576 | tf_op jit(solution)/shard_map/psum | solution.py:57
  458.5 0.0 copy-done.6
  458.6 0.9 stack.17
  459.5 14.8 %all-to-all-start = ((f32[64,8,384]{2,1,0:T(8,128)}), f32[64,8,384]{2,1,0:T(8,128)S(1)}, u32[]{:S(2)}, u32[]{:S(2)}) async-start(f32[64,8,384]{2,1,0:T(8,128)} %stack.17), calls=%async_computation | async-start | bytes 1572864 | tf_op jit(solution)/shard_map/all_to_all | solution.py:10
  474.3 0.6 maximum_bitcast_fusion
  475.0 22.4 %all-to-all-done = f32[64,8,384]{2,1,0:T(8,128)S(1)} async-done(((f32[64,8,384]{2,1,0:T(8,128)}), f32[64,8,384]{2,1,0:T(8,128)S(1)}, u32[]{:S(2)}, u32[]{:S(2)}) %all-to-all-start) | async-done | bytes 786464 | tf_op jit(solution)/shard_map/all_to_all | solution.py:10
  497.3 0.0 copy-done.5
  497.3 1.1 convolution_bitcast_fusion.1
  (2 shorter events, 0.0 us)
Async XLA Ops:
  7.2 10.3 %copy-start = (f32[1,1,4,512,256]{4,3,2,1,0:T(8,128)S(1)}, f32[1,1,4,512,256]{4,3,2,1,0:T(8,128)}, u32[]{:S(2)}) copy-start(f32[1,1,4,512,256]{4,3,2,1,0:T(8,128)} %param.12) | copy-start | bytes 6291460
  7.2 223.1 %all-reduce.2.cloned.1.call-start = ((), (), s32[]{:S(2)}) async-start(), calls=%async_computation.1 | async-start | bytes 6291456 | tf_op jit(solution)/shard_map/psum | solution.py:42
  23.1 207.2 %copy-start.2 = (f32[1,4,8,512]{3,2,1,0:T(8,128)S(1)}, f32[1,4,8,512]{3,2,1,0:T(8,128)}, u32[]{:S(2)}) copy-start(f32[1,4,8,512]{3,2,1,0:T(8,128)} %param.15) | copy-start | bytes 196612
  23.1 261.8 %copy-start.3 = (f32[1,3,8,512]{3,2,1,0:T(8,128)S(1)}, f32[1,3,8,512]{3,2,1,0:T(8,128)}, u32[]{:S(2)}) copy-start(f32[1,3,8,512]{3,2,1,0:T(8,128)} %param.16) | copy-start | bytes 147460
  230.3 104.0 %copy-start.1 = (f32[4,512,384]{1,2,0:T(8,128)S(1)}, f32[4,512,384]{1,2,0:T(8,128)}, u32[]{:S(2)}) copy-start(f32[4,512,384]{1,2,0:T(8,128)} %all-reduce.2.cloned.1.call-done) | copy-start | bytes 9437188
  285.0 149.4 %copy-start.4 = (f32[1,8,512]{2,1,0:T(8,128)S(1)}, f32[1,8,512]{2,1,0:T(8,128)}, u32[]{:S(2)}) copy-start(f32[1,8,512]{2,1,0:T(8,128)} %param.17) | copy-start | bytes 49156
  285.5 173.1 %copy-start.6 = (f32[8,384]{1,0:T(8,128)S(1)}, f32[8,384]{1,0:T(8,128)}, u32[]{:S(2)}) copy-start(f32[8,384]{1,0:T(8,128)} %param.18) | copy-start | bytes 36868
  335.6 161.8 %copy-start.5 = (f32[8,512]{1,0:T(8,128)S(1)}, f32[8,512]{1,0:T(8,128)}, u32[]{:S(2)}) copy-start(f32[8,512]{1,0:T(8,128)} %param.19) | copy-start | bytes 49156
  459.5 37.8 %all-to-all-start = ((f32[64,8,384]{2,1,0:T(8,128)}), f32[64,8,384]{2,1,0:T(8,128)S(1)}, u32[]{:S(2)}, u32[]{:S(2)}) async-start(f32[64,8,384]{2,1,0:T(8,128)} %stack.17), calls=%async_computation | async-start | bytes 1572864 | tf_op jit(solution)/shard_map/all_to_all | solution.py:10
Sparse Core Ops, SparseCore 0:
  23.3 206.9 all-reduce.1
